TPU v7x, 512 devices: a whole 4x8x8 slice. The times are simulated.
512 devices in a mesh: out: 16 (over y, core), in: 32 (over z, x).
Axes of the slice: x: 4, y: 8, z: 8, core: 2. Of those that a mesh axis runs over, the one named last changes fastest.
Arguments:
- weight: float32 [16384, 16384], P('out', 'in'), may hold values from -6 to 6
- keep_tiles: int32 [128, 128], P('out', 'in'), may hold values from 0 to 1, as said below
- factor_rows: float32 [4, 256, 16384], P(None, 'out', 'in'), may hold values from -0.375 to 0.375
- diag_inverse: float32 [16384], P('in'), may hold values from 0.5 to 2
- block_order: int32 [4], replicated, may hold values from 0 to 63, as said below
Outputs:
- pruned_weight: float32 [16384, 16384], P('out', 'in')
Inputs may be any that keep to these rules, and one draw needn't show every extreme that they name: `block_order`: distinct block numbers; the first and the last block are always among them. `keep_tiles`: for each index of out and each block of 256 inputs, the group of 16 tiles holds at most 10 zeros; in every block some group holds exactly 10.
All inputs are finite; a program needn't handle non-finite values.
Results may differ from a plain program's by a relative error of at most 0.0001.
Values sent between devices are 32-bit elements; how exact they have to be, the bound alone decides.
A program may use at most 64 MiB of HBM per device.

v0:
```python
import jax
import jax.numpy as jnp
from jax import lax
from jax.sharding import PartitionSpec as P

TILE = 128
NBLK = 4


def from_root(array, axis, root):
    mine = lax.axis_index(axis) == root
    return lax.psum(jnp.where(mine, array, jnp.zeros_like(array)), axis)


def expand_keep(flags):
    return jnp.repeat(jnp.repeat(flags, TILE, 0), TILE, 1)


def body(weight, keep_tiles, factor_rows, diag_inverse, block_order):
    rows, cols = weight.shape
    block = 2 * TILE
    per_device = cols // block
    col_ids = lax.axis_index("in") * cols + jnp.arange(cols, dtype=jnp.int32)
    col_block = col_ids // block
    keep_full = expand_keep(keep_tiles).astype(jnp.float32)
    panel_all = lax.all_gather(factor_rows, "out", axis=1, tiled=True)
    for step in range(NBLK):
        panel = panel_all[step]
        chosen_block = block_order[step]
        owner = chosen_block // per_device
        offset = chosen_block % per_device * block
        block_w = lax.dynamic_slice_in_dim(weight, offset, block, 1)
        block_keep = lax.dynamic_slice_in_dim(keep_full, offset, block, 1)
        scales = lax.dynamic_slice_in_dim(diag_inverse, offset, block, 0)
        errors = block_w * (1.0 - block_keep) * scales[None, :]
        errors = from_root(errors, "in", owner)
        update = jnp.dot(
            errors, panel, preferred_element_type=jnp.float32, precision=lax.Precision.HIGHEST
        )
        finished = jnp.any(col_block[:, None] == block_order[None, : step + 1], axis=1)
        weight = weight - jnp.where(finished[None, :], jnp.float32(0.0), update)
    processed = jnp.any(col_block[:, None] == block_order[None, :], axis=1)
    return jnp.where(processed[None, :], weight * keep_full, weight)


def solution(mesh):
    return jax.shard_map(
        body,
        mesh=mesh,
        in_specs=(P("out", "in"), P("out", "in"), P(None, "out", "in"), P("in"), P()),
        out_specs=P("out", "in"),
        check_vma=False,
    )
```

profile of v0, /device:TPU:8, one launch (start us, length us, event | category | flops | bytes accessed | tf_op | source)
XLA Modules:
  0.0 696.7 jit_solution(3402120489849063699)
XLA Ops:
  7.4 0.0 all-reduce.5.cloned.1.call-start
  7.4 1.5 fusion.4
  17.3 0.7 convert_element_type.11
  18.0 0.1 copy.7
  18.1 1.2 broadcast_in_dim.65
  19.4 0.0 copy-start.7
  19.4 1.5 copy.12
  20.9 0.0 copy-done.7
  20.9 0.1 fusion.3
  21.0 2.7 multiply_select_fusion.4
  23.6 0.0 all-reduce.5.cloned.1.call-update
  23.6 0.0 all-gather.2.cloned.1.call-start
  23.7 0.5 all-gather.2.cloned.1.call-update
  24.2 0.0 all-reduce.7.cloned.1.call-start
  25.0 0.6 broadcast_compare_fusion
  25.6 163.7 %all-reduce.5.cloned.1.call-done = f32[1024,256]{1,0:T(8,128)} async-done(((f32[1024,256]{1,0:T(8,128)}), f32[1024,256]{1,0:T(8,128)}) %all-reduce.5.cloned.1.call-update) | async-done | bytes 1048592 | tf_op jit(solution)/shard_map/psum | solution.py:12
  189.3 0.0 all-gather.2.cloned.1.call-done
  189.3 0.0 copy-start
  189.3 4.1 select_subtract_fusion.2
  193.4 0.0 copy-start.4
  193.4 1.3 copy-done.4
  194.7 0.0 copy-done
  194.7 0.0 copy-start.6
  194.7 1.3 multiply_select_fusion.3
  196.0 0.0 all-reduce.7.cloned.1.call-update
  196.0 0.0 all-reduce.9.cloned.1.call-start
  196.7 0.0 copy-done.6
  196.7 0.1 compare_reduce_fusion.1
  196.8 157.3 %all-reduce.7.cloned.1.call-done = f32[1024,256]{1,0:T(8,128)} async-done(((f32[1024,256]{1,0:T(8,128)}), f32[1024,256]{1,0:T(8,128)}) %all-reduce.7.cloned.1.call-update) | async-done | bytes 1048592 | tf_op jit(solution)/shard_map/psum | solution.py:12
  354.1 0.0 copy-start.1
  354.1 4.1 select_subtract_fusion.1
  358.3 0.0 copy-start.3
  358.3 1.3 copy-done.3
  359.6 0.0 copy-done.1
  359.6 1.3 multiply_select_fusion.2
  360.9 0.0 all-reduce.9.cloned.1.call-update
  360.9 0.0 all-reduce.11.cloned.1.call-start
  361.6 0.1 compare_reduce_fusion
  361.7 157.4 %all-reduce.9.cloned.1.call-done = f32[1024,256]{1,0:T(8,128)} async-done(((f32[1024,256]{1,0:T(8,128)}), f32[1024,256]{1,0:T(8,128)}) %all-reduce.9.cloned.1.call-update) | async-done | bytes 1048592 | tf_op jit(solution)/shard_map/psum | solution.py:12
  519.1 0.0 copy-start.2
  519.1 4.1 select_subtract_fusion
  523.3 0.0 copy-start.5
  523.3 1.3 copy-done.5
  524.6 0.0 copy-done.2
  524.6 1.2 multiply_select_fusion.1
  525.8 0.0 all-reduce.11.cloned.1.call-update
  525.8 0.1 compare_reduce_fusion.2
  525.9 158.2 %all-reduce.11.cloned.1.call-done = f32[1024,256]{1,0:T(8,128)} async-done(((f32[1024,256]{1,0:T(8,128)}), f32[1024,256]{1,0:T(8,128)}) %all-reduce.11.cloned.1.call-update) | async-done | bytes 1048592 | tf_op jit(solution)/shard_map/psum | solution.py:12
  684.1 5.4 multiply_select_fusion
  (2 shorter events, 0.0 us)
Async XLA Ops:
  7.4 181.9 %all-reduce.5.cloned.1.call-start = ((), (), s32[]{:S(2)}) async-start(), calls=%async_computation | async-start | bytes 2097152 | tf_op jit(solution)/shard_map/psum | solution.py:12
  19.4 1.5 copy-start.7
  23.6 165.6 %all-gather.2.cloned.1.call-start = ((), (), s32[]{:S(2)}) async-start(), calls=%async_computation.1 | async-start | bytes 2228224 | tf_op jit(solution)/shard_map/all_gather | solution.py:26
  24.2 329.9 %all-reduce.7.cloned.1.call-start = ((), (), s32[]{:S(2)}) async-start(), calls=%async_computation.2 | async-start | bytes 2097152 | tf_op jit(solution)/shard_map/psum | solution.py:12
  189.3 5.5 copy-start
  193.4 1.3 copy-start.4
  194.7 2.0 copy-start.6
  196.0 323.1 %all-reduce.9.cloned.1.call-start = ((), (), s32[]{:S(2)}) async-start(), calls=%async_computation.3 | async-start | bytes 2097152 | tf_op jit(solution)/shard_map/psum | solution.py:12
  354.1 5.5 copy-start.1
  358.3 1.3 copy-start.3
  360.9 323.2 %all-reduce.11.cloned.1.call-start = ((), (), s32[]{:S(2)}) async-start(), calls=%async_computation.4 | async-start | bytes 2097152 | tf_op jit(solution)/shard_map/psum | solution.py:12
  519.1 5.4 copy-start.2
  523.3 1.3 copy-start.5
Sparse Core Ops, SparseCore 0:
  23.8 165.4 all-reduce.4
  196.1 157.9 all-reduce.6
  361.0 158.0 all-reduce.8
  525.9 158.0 all-reduce.10
Sparse Core Ops, SparseCore 1:
  26.3 46.3 all-gather.1
where the time goes:
time: 697 us
  waiting for transfers between devices  637 us (91%)
  between operations  25.2 us (4%)
  matrix products  17.8 us (3%)
  local copies, waits for them, and re-layouts  8.32 us (1%)
  other arithmetic  8.03 us (1%)
    psum x4, waiting for transfers between devices, from_root(): return lax.psum(jnp.where(mine, array, jnp.zeros_like(array)), axis)  637 us
    dot_general x4, matrix products, body(): jnp.dot(errors, panel, preferred_element_type=jnp.float32, precision=lax....  17.8 us
  transfers between devices with their start and end apart: 5, of which 4 were waited for; matrix products, arithmetic and copies ran while one was open for 0% of the time, Pallas kernels for 0%

commit v1 on v0

--- a/solution.py
+++ b/solution.py
@@ -9,7 +9,7 @@
 
 def from_root(array, axis, root):
     mine = lax.axis_index(axis) == root
-    return lax.psum(jnp.where(mine, array, jnp.zeros_like(array)), axis)
+    return jnp.sum(lax.all_gather(jnp.where(mine, array, jnp.zeros_like(array)), axis), axis=0)
 
 
 def expand_keep(flags):

time: 697 us -> 1090 us (1.56)
  the two profiles are of different devices: /device:TPU:8 before, /device:TPU:1 now
where the time goes in v1:
time: 1090 us
  waiting for transfers between devices  982 us (90%)
  other arithmetic  55.7 us (5%)
  between operations  24.2 us (2%)
  matrix products  16.5 us (2%)
    all_gather x4, waiting for transfers between devices, from_root(): lax.all_gather(jnp.where(mine, array, jnp.zeros_like(array)), axis)  951 us
    reduce_sum x4, other arithmetic, from_root(): jnp.sum(lax.all_gather(jnp.where(mine, array, jnp.zeros_like(array)), axi...  47.7 us
    all_gather x1, waiting for transfers between devices, body(): panel_all = lax.all_gather(factor_rows, 'out', axis=1, tiled=True)  29.5 us
  transfers between devices with their start and end apart: 5, of which 5 were waited for; matrix products, arithmetic and copies ran while one was open for 1% of the time, Pallas kernels for 0%

profile of v1, /device:TPU:1, one launch (start us, length us, event | category | flops | bytes accessed | tf_op | source)
XLA Modules:
  0.0 1086.8 jit_solution(7353144856124484922)
XLA Ops:
  6.5 0.0 all-gather.12.cloned.1.call-start
  6.5 1.5 fusion.4
  16.9 0.7 convert_element_type.11
  17.6 0.1 copy.7
  17.7 1.2 broadcast_in_dim.65
  18.9 0.0 copy-start.7
  18.9 1.5 copy.12
  20.4 0.0 copy-done.7
  20.4 0.1 fusion.3
  20.5 2.7 multiply_select_fusion.4
  23.2 0.0 all-gather.12.cloned.1.call-update
  23.2 0.0 all-gather.10.cloned.1.call-start
  23.3 0.7 all-gather.10.cloned.1.call-update
  24.0 0.0 all-gather.14.cloned.1.call-start
  24.7 0.7 broadcast_compare_fusion
  25.4 242.6 %all-gather.12.cloned.1.call-done = f32[32768,256]{1,0:T(8,128)} async-done(((f32[1024,256]{1,0:T(8,128)}), f32[32768,256]{1,0:T(8,128)}) %all-gather.12.cloned.1.call-update) | async-done | bytes 33554448 | tf_op jit(solution)/shard_map/all_gather | solution.py:12
  268.1 11.9 %reduce_sum.36 = f32[1024,256]{1,0:T(8,128)S(1)} reduce(f32[32,1024,256]{2,1,0:T(8,128)} %bitcast.33, f32[]{:T(128)} %constant.81.clone.1), dimensions={0}, to_apply=%region_1.2 | reduce | flops 8126464 | bytes 34603012 | tf_op jit(solution)/shard_map/reduce_sum | solution.py:12
  280.0 29.5 %all-gather.10.cloned.1.call-done = f32[4,256,512]{2,1,0:T(8,128)} async-done(((f32[4,16,512]{2,1,0:T(8,128)}), f32[4,256,512]{2,1,0:T(8,128)}) %all-gather.10.cloned.1.call-update) | async-done | bytes 2097168 | tf_op jit(solution)/shard_map/all_gather | solution.py:26
  309.5 0.0 copy-start
  309.5 3.8 select_subtract_fusion.2
  313.3 0.0 copy-start.4
  313.3 1.4 copy-done.4
  314.7 0.0 copy-done
  314.7 0.0 copy-start.6
  314.7 1.2 multiply_select_fusion.3
  315.9 0.0 all-gather.14.cloned.1.call-update
  316.0 0.0 all-gather.16.cloned.1.call-start
  316.7 0.0 copy-done.6
  316.7 0.1 compare_reduce_fusion.1
  316.8 237.0 %all-gather.14.cloned.1.call-done = f32[32768,256]{1,0:T(8,128)} async-done(((f32[1024,256]{1,0:T(8,128)}), f32[32768,256]{1,0:T(8,128)}) %all-gather.14.cloned.1.call-update) | async-done | bytes 33554448 | tf_op jit(solution)/shard_map/all_gather | solution.py:12
  553.8 11.9 %reduce_sum.37 = f32[1024,256]{1,0:T(8,128)S(1)} reduce(f32[32,1024,256]{2,1,0:T(8,128)} %bitcast.35, f32[]{:T(128)} %constant.81.clone.1), dimensions={0}, to_apply=%region_3.4 | reduce | flops 8126464 | bytes 34603012 | tf_op jit(solution)/shard_map/reduce_sum | solution.py:12
  565.7 0.0 copy-start.1
  565.8 3.8 select_subtract_fusion.1
  569.6 0.0 copy-start.3
  569.6 1.4 copy-done.3
  570.9 0.0 copy-done.1
  571.0 1.2 multiply_select_fusion.2
  572.2 0.0 all-gather.16.cloned.1.call-update
  572.2 0.0 all-gather.18.cloned.1.call-start
  573.0 0.1 compare_reduce_fusion
  573.0 235.5 %all-gather.16.cloned.1.call-done = f32[32768,256]{1,0:T(8,128)} async-done(((f32[1024,256]{1,0:T(8,128)}), f32[32768,256]{1,0:T(8,128)}) %all-gather.16.cloned.1.call-update) | async-done | bytes 33554448 | tf_op jit(solution)/shard_map/all_gather | solution.py:12
  808.5 11.9 %reduce_sum.38 = f32[1024,256]{1,0:T(8,128)S(1)} reduce(f32[32,1024,256]{2,1,0:T(8,128)} %bitcast.34, f32[]{:T(128)} %constant.81.clone.1), dimensions={0}, to_apply=%region_5.6 | reduce | flops 8126464 | bytes 34603012 | tf_op jit(solution)/shard_map/reduce_sum | solution.py:12
  820.4 0.0 copy-start.2
  820.4 3.8 select_subtract_fusion
  824.3 0.0 copy-start.5
  824.3 1.4 copy-done.5
  825.6 0.0 copy-done.2
  825.6 1.2 multiply_select_fusion.1
  826.9 0.0 all-gather.18.cloned.1.call-update
  826.9 0.1 compare_reduce_fusion.2
  827.0 236.2 %all-gather.18.cloned.1.call-done = f32[32768,256]{1,0:T(8,128)} async-done(((f32[1024,256]{1,0:T(8,128)}), f32[32768,256]{1,0:T(8,128)}) %all-gather.18.cloned.1.call-update) | async-done | bytes 33554448 | tf_op jit(solution)/shard_map/all_gather | solution.py:12
  1063.2 11.9 %reduce_sum.39 = f32[1024,256]{1,0:T(8,128)S(1)} reduce(f32[32,1024,256]{2,1,0:T(8,128)} %bitcast.36, f32[]{:T(128)} %constant.81.clone.1), dimensions={0}, to_apply=%region_6.7 | reduce | flops 8126464 | bytes 34603012 | tf_op jit(solution)/shard_map/reduce_sum | solution.py:12
  1075.1 5.1 multiply_select_fusion
  (2 shorter events, 0.0 us)
Async XLA Ops:
  6.5 261.5 %all-gather.12.cloned.1.call-start = ((), (), s32[]{:S(2)}) async-start(), calls=%async_computation.1 | async-start | bytes 34603008 | tf_op jit(solution)/shard_map/all_gather | solution.py:12
  18.9 1.5 copy-start.7
  23.2 286.3 %all-gather.10.cloned.1.call-start = ((), (), s32[]{:S(2)}) async-start(), calls=%async_computation | async-start | bytes 2228224 | tf_op jit(solution)/shard_map/all_gather | solution.py:26
  24.0 529.9 %all-gather.14.cloned.1.call-start = ((), (), s32[]{:S(2)}) async-start(), calls=%async_computation.2 | async-start | bytes 34603008 | tf_op jit(solution)/shard_map/all_gather | solution.py:12
  309.5 5.2 copy-start
  313.3 1.4 copy-start.4
  314.7 2.0 copy-start.6
  316.0 492.5 %all-gather.16.cloned.1.call-start = ((), (), s32[]{:S(2)}) async-start(), calls=%async_computation.3 | async-start | bytes 34603008 | tf_op jit(solution)/shard_map/all_gather | solution.py:12
  565.7 5.2 copy-start.1
  569.6 1.4 copy-start.3
  572.2 491.0 %all-gather.18.cloned.1.call-start = ((), (), s32[]{:S(2)}) async-start(), calls=%async_computation.4 | async-start | bytes 34603008 | tf_op jit(solution)/shard_map/all_gather | solution.py:12
  820.4 5.2 copy-start.2
  824.3 1.4 copy-start.5
Sparse Core Ops, SparseCore 0:
  23.3 244.6 all-gather.11
  270.2 39.2 all-gather.9
  316.1 237.6 all-gather.13
  572.3 236.1 all-gather.15
  827.0 236.1 all-gather.17
